TPU v7x, 128 devices: a whole 4x4x4 slice. The times are simulated.
128 devices in a mesh: samp: 8 (over z, y_lo), seq: 16 (over x, y_hi, core).
Axes of the slice: x: 4, y: 4 (y_hi: 2, y_lo: 2; y = y_hi * 2 + y_lo), z: 4, core: 2. Of those that a mesh axis runs over, the one named last changes fastest.
Arguments:
- atom_in: bfloat16 [32, 4096, 128], P('samp', 'seq'), may hold values from -6 to 6
- tok_in: bfloat16 [32, 1024, 768], P('samp', 'seq'), may hold values from -6 to 6
- atom_cond: bfloat16 [4096, 128], P('seq'), may hold values from -6 to 6
- single_cond: bfloat16 [1024, 384], P('seq'), may hold values from -6 to 6
- atom_pair: bfloat16 [16, 4096, 128], P(None, 'seq'), may hold values from -6 to 6
- token_pair: bfloat16 [128, 1024, 1024], P(None, 'seq'), may hold values from -6 to 6
- atom_w_cond: bfloat16 [128, 768], replicated, may hold values from -0.5 to 0.5
- atom_w_qkvg: bfloat16 [128, 512], replicated, may hold values from -0.5 to 0.5
- atom_w_out: bfloat16 [128, 128], replicated, may hold values from -1.5 to 1.5
- atom_w_up: bfloat16 [128, 512], replicated, may hold values from -0.5 to 0.5
- atom_w_down: bfloat16 [256, 128], replicated, may hold values from -0.75 to 0.75
- atom_w_pair: bfloat16 [16, 4], replicated, may hold values from -1.5 to 1.5
- pool_weight: bfloat16 [128, 768], replicated, may hold values from -0.5 to 0.5
- token_w_cond: bfloat16 [384, 4608], replicated, may hold values from -0.3125 to 0.3125
- token_w_qkvg: bfloat16 [768, 3072], replicated, may hold values from -0.21875 to 0.21875
- token_w_out: bfloat16 [768, 768], replicated, may hold values from -0.625 to 0.625
- token_w_up: bfloat16 [768, 3072], replicated, may hold values from -0.21875 to 0.21875
- token_w_down: bfloat16 [1536, 768], replicated, may hold values from -0.3125 to 0.3125
- token_w_pair: bfloat16 [16, 128], replicated, may hold values from -0.5 to 0.5
- cotangent: bfloat16 [32, 1024, 768], P('samp', 'seq'), may hold values from -6 to 6
Outputs:
- token_out: bfloat16 [32, 1024, 768], P('samp', 'seq')
- grad_atom_in: float32 [32, 4096, 128], P('samp', 'seq')
- grad_tok_in: float32 [32, 1024, 768], P('samp', 'seq')
- grad_atom_w_cond: float32 [128, 768], P('seq')
- grad_atom_w_qkvg: float32 [128, 512], P('seq')
- grad_atom_w_out: float32 [128, 128], P('seq')
- grad_atom_w_up: float32 [128, 512], P('seq')
- grad_atom_w_down: float32 [256, 128], P('seq')
- grad_atom_w_pair: float32 [16, 4], P('seq')
- grad_pool_weight: float32 [128, 768], P('seq')
- grad_token_w_cond: float32 [384, 4608], P('seq')
- grad_token_w_qkvg: float32 [768, 3072], P('seq')
- grad_token_w_out: float32 [768, 768], P('seq')
- grad_token_w_up: float32 [768, 3072], P('seq')
- grad_token_w_down: float32 [1536, 768], P('seq')
- grad_token_w_pair: float32 [16, 128], P('seq')
All inputs are finite; a program needn't handle non-finite values.
Results may differ from a plain program's by a relative error of at most 0.025.
Values may be sent and summed in bfloat16 or wider, within the bound.
No kernel may reach another device: no remote copies, remote signals or barrier semaphores. Data moves between devices by JAX's collectives and lax.ppermute only.
A program may use at most 320 MiB of HBM per device.

v0:
```python
import functools
import math

import jax
import jax.numpy as jnp
from jax import lax
from jax.sharding import PartitionSpec as P

QWIN = 32
KWIN = 128


eps = 1e-05
masked = -1000000000.0


def with_halo(cells, sides, width):
    for axis, dim in sides:
        count = lax.axis_size(axis)
        ends = count - 1
        head = lax.slice_in_dim(cells, 0, width, axis=dim)
        tail = lax.slice_in_dim(cells, cells.shape[dim] - width, cells.shape[dim], axis=dim)
        cells = jnp.concatenate(
            [
                lax.ppermute(tail, axis, [(i, (i + 1) % count) for i in range(ends)]),
                cells,
                lax.ppermute(head, axis, [((i + 1) % count, i) for i in range(ends)]),
            ],
            axis=dim,
        )
    return cells


def shifted(value, axis, steps):
    count = lax.axis_size(axis)
    leading, last = (max(0, -steps), min(count, count - steps))
    return lax.ppermute(value, axis, [(source, source + steps) for source in range(leading, last)])


def for_sending(x):
    return jax.tree.map(lambda a: a.astype(jnp.bfloat16) if a.dtype == jnp.float32 else a, x)


def product(left, right):
    return jnp.dot(left, right, preferred_element_type=jnp.float32)


def product_right(left, right):
    return lax.dot_general(
        left, right, (((left.ndim - 1,), (1,)), ((), ())), preferred_element_type=jnp.float32
    )


def weight_grad(inputs, outputs):
    flat_in = inputs.reshape(-1, inputs.shape[-1])
    flat_out = outputs.reshape(-1, outputs.shape[-1])
    return lax.dot_general(
        flat_in, flat_out, (((0,), (0,)), ((), ())), preferred_element_type=jnp.float32
    )


def sig_slope(squashed):
    return squashed * (1.0 - squashed)


def norm_stats(x, axis):
    centred = x - jnp.mean(x, axis=axis, keepdims=True)
    inverse = lax.rsqrt(jnp.mean(centred * centred, axis=axis, keepdims=True) + eps)
    return (centred * inverse, inverse)


def norm_back(gradient, normed, inverse):
    return inverse * (
        gradient
        - jnp.mean(gradient, axis=-1, keepdims=True)
        - normed * jnp.mean(gradient * normed, axis=-1, keepdims=True)
    )


def window_keys(padded, n_windows):
    rim_width = (KWIN - QWIN) // 2
    block_rows = math.gcd(QWIN, rim_width)
    stride = QWIN // block_rows
    blocks = padded.reshape(padded.shape[0], -1, block_rows, padded.shape[-1])
    pieces = [blocks[:, m : m + stride * n_windows : stride] for m in range(KWIN // block_rows)]
    return jnp.concatenate(pieces, axis=2)


def window_back(grad_windows, n_windows, length):
    rim_width = (KWIN - QWIN) // 2
    block_rows = math.gcd(QWIN, rim_width)
    stride = QWIN // block_rows
    sample_count = grad_windows.shape[0]
    channels = grad_windows.shape[-1]
    blocks = jnp.zeros((sample_count, length // block_rows, block_rows, channels), jnp.float32)
    for m in range(KWIN // block_rows):
        blocks = blocks.at[:, m : m + stride * n_windows : stride].add(
            grad_windows[:, :, m * block_rows : (m + 1) * block_rows]
        )
    return blocks.reshape(sample_count, length, channels)


def token_scores(query_heads, key_heads, score_bias):
    head_size = query_heads.shape[-1]
    return (
        jnp.einsum("sqhd,skhd->shqk", query_heads, key_heads, preferred_element_type=jnp.float32)
        * head_size ** (-0.5)
        + score_bias[None]
    )


def token_forward(query_part, key_part, value_part, score_bias, head_count):
    sample_count, row_count, channels = query_part.shape
    head_size = channels // head_count
    joined = jnp.concatenate([key_part, value_part], axis=-1)
    gathered = lax.all_gather(joined, "seq", axis=1, tiled=True)
    key_heads = gathered[..., :channels].reshape(sample_count, -1, head_count, head_size)
    value_heads = gathered[..., channels:].reshape(sample_count, -1, head_count, head_size)
    query_heads = query_part.reshape(sample_count, row_count, head_count, head_size)
    scores = token_scores(query_heads, key_heads, score_bias)
    row_max = jnp.max(scores, axis=-1, keepdims=True)
    exponent = jnp.exp(scores - row_max)
    row_total = jnp.sum(exponent, axis=-1, keepdims=True)
    attention = (exponent / row_total).astype(jnp.bfloat16)
    attended = jnp.einsum(
        "shqk,skhd->sqhd", attention, value_heads, preferred_element_type=jnp.float32
    )
    log_total = row_max + jnp.log(row_total)
    return (
        attended.reshape(sample_count, row_count, channels),
        (query_heads, key_heads, value_heads, log_total),
    )


def token_backward(grad_attended, stored, score_bias, pair_low, head_count):
    query_heads, key_heads, value_heads, log_total = stored
    sample_count, row_count, channels = grad_attended.shape
    head_size = channels // head_count
    score_scale = head_size ** (-0.5)
    grad_heads = grad_attended.reshape(query_heads.shape)
    attention = jnp.exp(token_scores(query_heads, key_heads, score_bias) - log_total)
    grad_attention = jnp.einsum(
        "sqhd,skhd->shqk", grad_heads, value_heads, preferred_element_type=jnp.float32
    )
    row_dot = jnp.sum(attention * grad_attention, axis=-1, keepdims=True)
    grad_scores = (attention * (grad_attention - row_dot)).astype(jnp.bfloat16)
    grad_query = (
        jnp.einsum("shqk,skhd->sqhd", grad_scores, key_heads, preferred_element_type=jnp.float32)
        * score_scale
    )
    grad_keys = (
        jnp.einsum("shqk,sqhd->skhd", grad_scores, query_heads, preferred_element_type=jnp.float32)
        * score_scale
    )
    grad_values = jnp.einsum(
        "shqk,sqhd->skhd",
        attention.astype(jnp.bfloat16),
        grad_heads,
        preferred_element_type=jnp.float32,
    )
    grad_pair = jnp.einsum(
        "shqk,cqk->hc", grad_scores, pair_low, preferred_element_type=jnp.float32
    )
    grad_joined = jnp.concatenate(
        [
            grad_keys.reshape(sample_count, -1, channels),
            grad_values.reshape(sample_count, -1, channels),
        ],
        axis=-1,
    )
    own_grads = lax.psum_scatter(
        grad_joined.astype(jnp.bfloat16), "seq", scatter_dimension=1, tiled=True
    ).astype(jnp.float32)
    return (
        grad_query.reshape(sample_count, row_count, channels),
        own_grads[..., :channels],
        own_grads[..., channels:],
        grad_pair,
    )


def atom_scores(query_heads, key_heads, score_bias, key_valid):
    head_size = query_heads.shape[-1]
    raw = (
        jnp.einsum("swqhd,swkhd->swhqk", query_heads, key_heads, preferred_element_type=jnp.float32)
        * head_size ** (-0.5)
        + score_bias[None]
    )
    return jnp.where(key_valid[None, :, None, None, :], raw, masked)


def atom_forward(query_part, key_part, value_part, score_bias, key_valid, head_count):
    sample_count, row_count, channels = query_part.shape
    head_size = channels // head_count
    n_windows = row_count // QWIN
    rim_width = (KWIN - QWIN) // 2
    joined = jnp.concatenate([key_part, value_part], axis=-1)
    padded = with_halo(joined, (("seq", 1),), rim_width)
    windows = window_keys(padded, n_windows)
    key_heads = windows[..., :channels].reshape(
        sample_count, n_windows, KWIN, head_count, head_size
    )
    value_heads = windows[..., channels:].reshape(
        sample_count, n_windows, KWIN, head_count, head_size
    )
    query_heads = query_part.reshape(sample_count, n_windows, QWIN, head_count, head_size)
    scores = atom_scores(query_heads, key_heads, score_bias, key_valid)
    row_max = jnp.max(scores, axis=-1, keepdims=True)
    exponent = jnp.exp(scores - row_max)
    row_total = jnp.sum(exponent, axis=-1, keepdims=True)
    attention = (exponent / row_total).astype(jnp.bfloat16)
    attended = jnp.einsum(
        "swhqk,swkhd->swqhd", attention, value_heads, preferred_element_type=jnp.float32
    )
    log_total = row_max + jnp.log(row_total)
    return (
        attended.reshape(sample_count, row_count, channels),
        (query_heads, key_heads, value_heads, log_total),
    )


def atom_backward(grad_attended, stored, score_bias, key_valid, pair_low, head_count):
    query_heads, key_heads, value_heads, log_total = stored
    sample_count, row_count, channels = grad_attended.shape
    head_size = channels // head_count
    n_windows = row_count // QWIN
    rim_width = (KWIN - QWIN) // 2
    score_scale = head_size ** (-0.5)
    grad_heads = grad_attended.reshape(query_heads.shape)
    attention = jnp.exp(atom_scores(query_heads, key_heads, score_bias, key_valid) - log_total)
    grad_attention = jnp.einsum(
        "swqhd,swkhd->swhqk", grad_heads, value_heads, preferred_element_type=jnp.float32
    )
    row_dot = jnp.sum(attention * grad_attention, axis=-1, keepdims=True)
    grad_scores = (attention * (grad_attention - row_dot)).astype(jnp.bfloat16)
    grad_query = (
        jnp.einsum("swhqk,swkhd->swqhd", grad_scores, key_heads, preferred_element_type=jnp.float32)
        * score_scale
    )
    grad_keys = (
        jnp.einsum(
            "swhqk,swqhd->swkhd", grad_scores, query_heads, preferred_element_type=jnp.float32
        )
        * score_scale
    )
    grad_values = jnp.einsum(
        "swhqk,swqhd->swkhd",
        attention.astype(jnp.bfloat16),
        grad_heads,
        preferred_element_type=jnp.float32,
    )
    grad_pair = jnp.einsum(
        "swhqk,cwqk->ch", grad_scores, pair_low, preferred_element_type=jnp.float32
    )
    grad_windows = jnp.concatenate(
        [
            grad_keys.reshape(sample_count, n_windows, KWIN, channels),
            grad_values.reshape(sample_count, n_windows, KWIN, channels),
        ],
        axis=-1,
    )
    grad_padded = window_back(grad_windows, n_windows, row_count + 2 * rim_width)
    own_grads = grad_padded[:, rim_width : rim_width + row_count]
    from_next = shifted(grad_padded[:, :rim_width].astype(jnp.bfloat16), "seq", -1).astype(
        jnp.float32
    )
    from_prev = shifted(
        grad_padded[:, rim_width + row_count :].astype(jnp.bfloat16), "seq", 1
    ).astype(jnp.float32)
    own_grads = own_grads.at[:, row_count - rim_width :].add(from_next)
    own_grads = own_grads.at[:, :rim_width].add(from_prev)
    return (
        grad_query.reshape(sample_count, row_count, channels),
        own_grads[..., :channels],
        own_grads[..., channels:],
        grad_pair,
    )


def block_forward(x, cond_low, weights, attend):
    cond_weight, qkvg_weight, out_weight, up_weight, down_weight = weights
    channels = x.shape[-1]
    cond_proj = product(cond_low, cond_weight)[None]
    cond_parts = [cond_proj[..., i * channels : (i + 1) * channels] for i in range(6)]
    normed_a, inverse_a = norm_stats(x, -1)
    scale_a = jax.nn.sigmoid(cond_parts[0])
    first_low = (scale_a * normed_a + cond_parts[1]).astype(jnp.bfloat16)
    projected = product(first_low, qkvg_weight)
    qkv_low = projected[..., : 3 * channels].astype(jnp.bfloat16)
    gate_sig = jax.nn.sigmoid(projected[..., 3 * channels :])
    attended, kept_attn = attend(
        qkv_low[..., :channels], qkv_low[..., channels : 2 * channels], qkv_low[..., 2 * channels :]
    )
    gated_low = (gate_sig * attended).astype(jnp.bfloat16)
    branch = product(gated_low, out_weight)
    gate_a = jax.nn.sigmoid(cond_parts[2])
    middle = x + gate_a * branch
    normed_b, inverse_b = norm_stats(middle, -1)
    scale_b = jax.nn.sigmoid(cond_parts[3])
    second_low = (scale_b * normed_b + cond_parts[4]).astype(jnp.bfloat16)
    up_out = product(second_low, up_weight)
    hidden_width = up_out.shape[-1] // 2
    gate_half = up_out[..., :hidden_width]
    up_half = up_out[..., hidden_width:]
    half_sig = jax.nn.sigmoid(gate_half)
    hidden_low = (gate_half * half_sig * up_half).astype(jnp.bfloat16)
    down_out = product(hidden_low, down_weight)
    gate_b = jax.nn.sigmoid(cond_parts[5])
    stored = (
        normed_a,
        inverse_a,
        scale_a,
        first_low,
        gate_sig,
        attended,
        kept_attn,
        gated_low,
        branch,
        gate_a,
        normed_b,
        inverse_b,
        scale_b,
        second_low,
        gate_half,
        up_half,
        half_sig,
        hidden_low,
        down_out,
        gate_b,
    )
    return (middle + gate_b * down_out, stored)


def block_backward(upstream, stored, cond_low, weights, attend_back):
    cond_weight, qkvg_weight, out_weight, up_weight, down_weight = weights
    (
        normed_a,
        inverse_a,
        scale_a,
        first_low,
        gate_sig,
        attended,
        kept_attn,
        gated_low,
        branch,
        gate_a,
        normed_b,
        inverse_b,
        scale_b,
        second_low,
        gate_half,
        up_half,
        half_sig,
        hidden_low,
        down_out,
        gate_b,
    ) = stored
    grad_gate_b = upstream * down_out * sig_slope(gate_b)
    grad_down = (upstream * gate_b).astype(jnp.bfloat16)
    grad_hidden = product_right(grad_down, down_weight)
    grad_gate_half = grad_hidden * up_half * half_sig * (1.0 + gate_half * (1.0 - half_sig))
    grad_up_half = grad_hidden * gate_half * half_sig
    grad_up = jnp.concatenate([grad_gate_half, grad_up_half], axis=-1).astype(jnp.bfloat16)
    grad_second = product_right(grad_up, up_weight)
    grad_scale_b = grad_second * normed_b * sig_slope(scale_b)
    grad_middle = upstream + norm_back(grad_second * scale_b, normed_b, inverse_b)
    grad_gate_a = grad_middle * branch * sig_slope(gate_a)
    grad_branch = (grad_middle * gate_a).astype(jnp.bfloat16)
    grad_gated = product_right(grad_branch, out_weight)
    grad_gates = grad_gated * attended * sig_slope(gate_sig)
    grad_attended = (grad_gated * gate_sig).astype(jnp.bfloat16)
    grad_query, grad_keys, grad_values, grad_pair = attend_back(grad_attended, kept_attn)
    grad_projected = jnp.concatenate(
        [grad_query, grad_keys, grad_values, grad_gates], axis=-1
    ).astype(jnp.bfloat16)
    grad_first = product_right(grad_projected, qkvg_weight)
    grad_scale_a = grad_first * normed_a * sig_slope(scale_a)
    grad_x = grad_middle + norm_back(grad_first * scale_a, normed_a, inverse_a)
    grad_cond = jnp.concatenate(
        [grad_scale_a, grad_first, grad_gate_a, grad_scale_b, grad_second, grad_gate_b], axis=-1
    ).astype(jnp.bfloat16)
    grad_cond_weight = jnp.einsum(
        "rc,srn->cn", cond_low, grad_cond, preferred_element_type=jnp.float32
    )
    return (
        grad_x,
        (
            grad_cond_weight,
            weight_grad(first_low, grad_projected),
            weight_grad(gated_low, grad_branch),
            weight_grad(second_low, grad_up),
            weight_grad(hidden_low, grad_down),
            grad_pair,
        ),
    )


def body(
    atom_in,
    tok_in,
    atom_cond,
    single_cond,
    atom_pair,
    token_pair,
    atom_w_cond,
    atom_w_qkvg,
    atom_w_out,
    atom_w_up,
    atom_w_down,
    atom_w_pair,
    pool_weight,
    token_w_cond,
    token_w_qkvg,
    token_w_out,
    token_w_up,
    token_w_down,
    token_w_pair,
    cotangent,
):
    sample_count, atom_rows, atom_width = atom_in.shape
    tok_rows = tok_in.shape[1]
    n_windows = atom_rows // QWIN
    rim_width = (KWIN - QWIN) // 2
    atom_low = norm_stats(atom_cond.astype(jnp.float32), -1)[0].astype(jnp.bfloat16)
    single_low = norm_stats(single_cond.astype(jnp.float32), -1)[0].astype(jnp.bfloat16)
    atom_pair_low = (
        norm_stats(atom_pair.astype(jnp.float32), 0)[0]
        .astype(jnp.bfloat16)
        .reshape(atom_pair.shape[0], n_windows, QWIN, KWIN)
    )
    token_pair_low = norm_stats(token_pair.astype(jnp.float32), 0)[0].astype(jnp.bfloat16)
    atom_bias = jnp.einsum(
        "cwqk,ch->whqk", atom_pair_low, atom_w_pair, preferred_element_type=jnp.float32
    )
    token_bias = jnp.einsum(
        "cqk,hc->hqk", token_pair_low, token_w_pair, preferred_element_type=jnp.float32
    )
    window_index = lax.axis_index("seq") * n_windows + jnp.arange(n_windows, dtype=jnp.int32)
    key_index = (
        QWIN * window_index[:, None] - rim_width + jnp.arange(KWIN, dtype=jnp.int32)[None, :]
    )
    key_valid = (key_index >= 0) & (key_index < atom_rows * lax.axis_size("seq"))
    atom_heads = atom_w_pair.shape[1]
    token_heads = token_w_pair.shape[0]
    atom_fwd = functools.partial(
        atom_forward, score_bias=atom_bias, key_valid=key_valid, head_count=atom_heads
    )
    atom_bwd = functools.partial(
        atom_backward,
        score_bias=atom_bias,
        key_valid=key_valid,
        pair_low=atom_pair_low,
        head_count=atom_heads,
    )
    token_fwd = functools.partial(token_forward, score_bias=token_bias, head_count=token_heads)
    token_bwd = functools.partial(
        token_backward, score_bias=token_bias, pair_low=token_pair_low, head_count=token_heads
    )
    atom_weights = (atom_w_cond, atom_w_qkvg, atom_w_out, atom_w_up, atom_w_down)
    token_weights = (token_w_cond, token_w_qkvg, token_w_out, token_w_up, token_w_down)
    atom_out, atom_stored = block_forward(
        atom_in.astype(jnp.float32), atom_low, atom_weights, atom_fwd
    )
    per_token = atom_rows // tok_rows
    pooled_low = jnp.mean(
        atom_out.reshape(sample_count, tok_rows, per_token, atom_width), axis=2
    ).astype(jnp.bfloat16)
    token_start = tok_in.astype(jnp.float32) + product(pooled_low, pool_weight)
    token_out, token_stored = block_forward(token_start, single_low, token_weights, token_fwd)
    grad_start, token_grads = block_backward(
        cotangent.astype(jnp.float32), token_stored, single_low, token_weights, token_bwd
    )
    grad_pool = grad_start.astype(jnp.bfloat16)
    grad_pooled = product_right(grad_pool, pool_weight) / per_token
    grad_atom_out = jnp.broadcast_to(
        grad_pooled[:, :, None, :], (sample_count, tok_rows, per_token, atom_width)
    ).reshape(sample_count, atom_rows, atom_width)
    grad_atoms, atom_grads = block_backward(
        grad_atom_out, atom_stored, atom_low, atom_weights, atom_bwd
    )
    all_grads = atom_grads + (weight_grad(pooled_low, grad_pool),) + token_grads
    summed = jax.tree.map(
        lambda part: part.astype(jnp.float32), lax.psum(for_sending(all_grads), "samp")
    )
    shares = jax.tree.map(
        lambda part: part.astype(jnp.float32),
        lax.psum_scatter(for_sending(summed), "seq", scatter_dimension=0, tiled=True),
    )
    return (token_out.astype(jnp.bfloat16), grad_atoms, grad_start) + tuple(shares)


def solution(mesh):
    in_specs = (
        P("samp", "seq", None),
        P("samp", "seq", None),
        P("seq", None),
        P("seq", None),
        P(None, "seq", None),
        P(None, "seq", None),
        P(),
        P(),
        P(),
        P(),
        P(),
        P(),
        P(),
        P(),
        P(),
        P(),
        P(),
        P(),
        P(),
        P("samp", "seq", None),
    )
    out_specs = (
        P("samp", "seq", None),
        P("samp", "seq", None),
        P("samp", "seq", None),
        P("seq", None),
        P("seq", None),
        P("seq", None),
        P("seq", None),
        P("seq", None),
        P("seq", None),
        P("seq", None),
        P("seq", None),
        P("seq", None),
        P("seq", None),
        P("seq", None),
        P("seq", None),
        P("seq", None),
    )
    return jax.shard_map(body, mesh=mesh, in_specs=in_specs, out_specs=out_specs, check_vma=False)
```

profile of v0, /device:TPU:0, one launch (start us, length us, event | category | flops | bytes accessed | tf_op | source)
XLA Modules:
  0.0 1255.4 jit_solution(13114210121173654885)
XLA Ops:
  74.9 9.6 fusion.2
  93.0 27.7 %fusion.32 = f32[16,64,1024]{2,0,1:T(8,128)S(1)} fusion(bf16[128,64,1024]{2,1,0:T(8,128)(2,1)} %fusion.3, bf16[16,128]{1,0:T(8,128)(2,1)S(1)} %copy-done.132), kind=kOutput, calls=%fused_computation.72 | convolution fusion | flops 268435456 | bytes 20975616 | tf_op jit(solution)/shard_map/cqk,hc->hqk/dot_general | solution.py:435
  125.6 38.0 %all-gather.2.cloned.1.call-done = bf16[4,1024,1536]{2,1,0:T(8,128)(2,1)} async-done(((bf16[4,64,1536]{2,1,0:T(8,128)(2,1)}), bf16[4,1024,1536]{2,1,0:T(8,128)(2,1)}) %all-gather.2.cloned.1.call-update) | async-done | bytes 12582928 | tf_op jit(solution)/shard_map/all_gather | solution.py:116
  163.6 10.2 fusion.214
  191.1 12.4 fusion.222
  237.7 13.8 %multiply_reduce_fusion = (f32[4,16,64]{2,1,0:T(8,128)S(1)}, f32[4,16,64,1024]{3,2,1,0:T(8,128)}) fusion(f32[4,16,64,1024]{3,2,1,0:T(8,128)} %get-tuple-element.131, f32[4,16,64]{2,1,0:T(8,128)S(1)} %copy-done.85, bf16[4,64,16,48]{1,3,2,0:T(8,128)(2,1)S(1)} %bitcast.295, bf16[4,1024,16,48]{1,3,2,0:T(8,128)(2,1)} %bitcast.285), kind=kOutput, calls=%fused_computation.16 | convolution fusion | flops 415232000 | bytes 40271872 | tf_op jit(solution)/shard_map/sqhd,skhd->shqk/dot_general | solution.py:142
  251.5 8.9 fusion.23
  260.4 14.0 %convert_reduce_fusion.1 = (bf16[16,64,1024]{2,1,0:T(8,128)(2,1)}, bf16[4,16,64,1024]{3,2,1,0:T(8,128)(2,1)S(1)}) fusion(f32[4,16,64,1024]{3,2,1,0:T(8,128)} %get-tuple-element.136, f32[4,16,64]{2,1,0:T(8,128)S(1)} %get-tuple-element.135, f32[4,16,64,1024]{3,2,1,0:T(8,128)} %get-tuple-element.131, f32[4,16,64]{2,1,0:T(8,128)S(1)} %copy-done.85), kind=kLoop, calls=%fused_computation.14 | loop fusion | flops 24117248 | bytes 44072960 | tf_op jit(solution)/shard_map/shqk,cqk->hc/reduce_sum | solution.py:161
  279.6 8.6 copy.131
  296.8 10.4 pad_maximum_fusion
  320.9 9.6 multiply_convert_fusion.4
  331.6 95.8 %reduce-scatter.12.cloned.1.call-done = bf16[4,64,1536]{2,1,0:T(8,128)(2,1)} async-done(((bf16[4,1024,1536]{2,1,0:T(8,128)(2,1)}), bf16[4,64,1536]{2,1,0:T(8,128)(2,1)}) %reduce-scatter.12.cloned.1.call-update) | async-done | bytes 786448 | tf_op jit(solution)/shard_map/reduce_scatter | solution.py:171
  449.6 26.8 %fusion.54 = bf16[16,128]{1,0:T(8,128)(2,1)} fusion(bf16[128,64,1024]{2,1,0:T(8,128)(2,1)} %fusion.3, bf16[16,64,1024]{2,1,0:T(8,128)(2,1)} %get-tuple-element.64), kind=kOutput, calls=%fused_computation.120 | convolution fusion | flops 268435456 | bytes 18878464 | tf_op jit(solution)/shard_map/shqk,cqk->hc/dot_general | solution.py:161
  557.0 67.2 %all-reduce.3 = (bf16[128,128]{1,0:T(8,128)(2,1)S(1)}, bf16[16,4]{1,0:T(8,128)(2,1)S(1)}, bf16[16,128]{1,0:T(8,128)(2,1)S(1)}) all-reduce(bf16[128,128]{1,0:T(8,128)(2,1)S(1)} %fusion.48, bf16[16,4]{1,0:T(8,128)(2,1)S(1)} %fusion.59, bf16[16,128]{1,0:T(8,128)(2,1)S(1)} %copy-done.129), channel_id=5, replica_groups=mesh['samp'=8,'seq'=16] {'seq'}, use_global_device_ids=true, to_apply=%region_46.47.clone | all-reduce | flops 18496 | bytes 73984
  624.2 34.3 %reduce-scatter.30.cloned.1.call-done = bf16[48,3072]{1,0:T(8,128)(2,1)} async-done(((bf16[768,3072]{1,0:T(8,128)(2,1)}), bf16[48,3072]{1,0:T(8,128)(2,1)}) %reduce-scatter.30.cloned.1.call-update) | async-done | bytes 294928 | tf_op jit(solution)/shard_map/reduce_scatter | solution.py:487
  658.5 80.4 %reduce-scatter.24.cloned.1.call-done = bf16[24,4608]{1,0:T(8,128)(2,1)} async-done(((bf16[384,4608]{1,0:T(8,128)(2,1)}), bf16[24,4608]{1,0:T(8,128)(2,1)}) %reduce-scatter.24.cloned.1.call-update) | async-done | bytes 221200 | tf_op jit(solution)/shard_map/reduce_scatter | solution.py:487
  738.9 86.2 %reduce-scatter.26.cloned.1.call-done = bf16[48,3072]{1,0:T(8,128)(2,1)} async-done(((bf16[768,3072]{1,0:T(8,128)(2,1)}), bf16[48,3072]{1,0:T(8,128)(2,1)}) %reduce-scatter.26.cloned.1.call-update) | async-done | bytes 294928 | tf_op jit(solution)/shard_map/reduce_scatter | solution.py:487
  830.7 58.5 %reduce-scatter.20.cloned.1.call-done = bf16[16,128]{1,0:T(8,128)(2,1)} async-done(((bf16[256,128]{1,0:T(8,128)(2,1)}), bf16[16,128]{1,0:T(8,128)(2,1)}) %reduce-scatter.20.cloned.1.call-update) | async-done | bytes 4112 | tf_op jit(solution)/shard_map/reduce_scatter | solution.py:487
  889.2 67.6 %reduce-scatter.18.cloned.1.call-done = bf16[8,512]{1,0:T(8,128)(2,1)} async-done(((bf16[128,512]{1,0:T(8,128)(2,1)}), bf16[8,512]{1,0:T(8,128)(2,1)}) %reduce-scatter.18.cloned.1.call-update) | async-done | bytes 8208 | tf_op jit(solution)/shard_map/reduce_scatter | solution.py:487
  956.8 67.9 %reduce-scatter.16.cloned.1.call-done = bf16[8,512]{1,0:T(8,128)(2,1)} async-done(((bf16[128,512]{1,0:T(8,128)(2,1)}), bf16[8,512]{1,0:T(8,128)(2,1)}) %reduce-scatter.16.cloned.1.call-update) | async-done | bytes 8208 | tf_op jit(solution)/shard_map/reduce_scatter | solution.py:487
  1024.7 66.1 %reduce-scatter.22.cloned.1.call-done = bf16[8,768]{1,0:T(8,128)(2,1)} async-done(((bf16[128,768]{1,0:T(8,128)(2,1)}), bf16[8,768]{1,0:T(8,128)(2,1)}) %reduce-scatter.22.cloned.1.call-update) | async-done | bytes 12304 | tf_op jit(solution)/shard_map/reduce_scatter | solution.py:487
  1090.8 66.7 %reduce-scatter.14.cloned.1.call-done = bf16[8,768]{1,0:T(8,128)(2,1)} async-done(((bf16[128,768]{1,0:T(8,128)(2,1)}), bf16[8,768]{1,0:T(8,128)(2,1)}) %reduce-scatter.14.cloned.1.call-update) | async-done | bytes 12304 | tf_op jit(solution)/shard_map/reduce_scatter | solution.py:487
  1157.4 36.5 %all-reduce.4 = (bf16[8,768]{1,0:T(8,128)(2,1)}, bf16[8,512]{1,0:T(8,128)(2,1)}, bf16[8,128]{1,0:T(8,128)(2,1)}, bf16[8,512]{1,0:T(8,128)(2,1)}, bf16[16,128]{1,...) all-reduce(bf16[8,768]{1,0:T(8,128)(2,1)} %reduce-scatter.14.cloned, ...), channel_id=1, replica_groups=mesh['samp'=8,'seq'=16] {'samp'}, use_global_device_ids=true, to_apply=%region_41.42 | all-reduce | flops 23684 | bytes 94736 | tf_op jit(solution)/shard_map/psum | solution.py:483
  1202.7 39.0 %all-reduce.8.cloned.1.call-done = (bf16[24,4608]{1,0:T(8,128)(2,1)}, bf16[48,3072]{1,0:T(8,128)(2,1)}, bf16[48,768]{1,0:T(8,128)(2,1)}, bf16[48,3072]{1,0:T(8,128)(2,1)}, bf16[96,768]{1,0:T(8,128)(2,1)}) async-done(((bf16[24,4608]{1,0:T(8,128)(2,1)}, bf16[48,3072]{1,0:T(8,128)(2,1)}, bf16[48,768]{1,0:T(8,128)(2,1)}, bf16[48,3072]{1,0:T(8,128)(2,1)}, bf16[96,768]{1,0:T(8,128)(2,1)}), ...) | async-done | bytes 1032208 | tf_op jit(solution)/shard_map/psum | solution.py:483
  (545 shorter events, 282.0 us)
Async XLA Ops:
  7.2 156.4 %all-gather.2.cloned.1.call-start = ((), (), s32[]{:S(2)}) async-start(), calls=%async_computation.11 | async-start | bytes 13369344 | tf_op jit(solution)/shard_map/all_gather | solution.py:116
  15.9 16.4 %collective-permute-start = (bf16[4,48,256]{2,1,0:T(8,128)(2,1)}, bf16[4,48,256]{2,1,0:T(8,128)(2,1)}, u32[]{:S(2)}, u32[]{:S(2)}) collective-permute-start(bf16[4,48,256]{2,1,0:T(8,128)(2,1)} %get-tuple-element.103), channel_id=1, source_target_pairs={{0,1},{1,2},{2,3},{3,4},{4,5},{5,6},{6,7},{7,8},{8,9},{9,10},{10,1... | collective-permute-start | bytes 294920 | tf_op jit(solution)/shard_map/ppermute | solution.py:25
  17.8 14.5 %collective-permute-start.1 = (bf16[4,48,256]{2,1,0:T(8,128)(2,1)}, bf16[4,48,256]{2,1,0:T(8,128)(2,1)}, u32[]{:S(2)}, u32[]{:S(2)}) collective-permute-start(bf16[4,48,256]{2,1,0:T(8,128)(2,1)} %get-tuple-element.104), channel_id=1, source_target_pairs={{1,0},{2,1},{3,2},{4,3},{5,4},{6,5},{7,6},{8,7},{9,8},{10,9},{11,1... | collective-permute-start | bytes 294920 | tf_op jit(solution)/shard_map/ppermute | solution.py:27
  66.2 361.2 %reduce-scatter.12.cloned.1.call-start = ((), (), s32[]{:S(2)}) async-start(), calls=%async_computation.12 | async-start | bytes 13369344 | tf_op jit(solution)/shard_map/reduce_scatter | solution.py:171
  125.6 65.5 %copy-start.26 = (bf16[4,64,768]{1,2,0:T(8,128)(2,1)}, bf16[4,64,768]{1,2,0:T(8,128)(2,1)S(1)}, u32[]{:S(2)}) copy-start(bf16[4,64,768]{1,2,0:T(8,128)(2,1)S(1)} %copy.171) | copy-start | bytes 1179652
  307.3 316.9 %reduce-scatter.28.cloned.1.call-start = ((), (), s32[]{:S(2)}) async-start(), calls=%async_computation.20 | async-start | bytes 1253376 | tf_op jit(solution)/shard_map/reduce_scatter | solution.py:487
  311.0 313.2 %reduce-scatter.32.cloned.1.call-start = ((), (), s32[]{:S(2)}) async-start(), calls=%async_computation.22 | async-start | bytes 2506752 | tf_op jit(solution)/shard_map/reduce_scatter | solution.py:487
  314.5 344.1 %reduce-scatter.30.cloned.1.call-start = ((), (), s32[]{:S(2)}) async-start(), calls=%async_computation.21 | async-start | bytes 5013504 | tf_op jit(solution)/shard_map/reduce_scatter | solution.py:487
  320.8 106.6 %copy-start.52 = (f32[64,768]{1,0:T(8,128)S(1)}, f32[64,768]{1,0:T(8,128)}, u32[]{:S(2)}) copy-start(f32[64,768]{1,0:T(8,128)} %copy-done.51) | copy-start | bytes 589828
  320.8 106.6 %copy-start.118 = (f32[4,64]{1,0:T(4,128)S(1)}, f32[4,64]{1,0:T(4,128)}, u32[]{:S(2)}) copy-start(f32[4,64]{1,0:T(4,128)} %copy-done.117) | copy-start | bytes 3076
  320.8 106.6 %copy-start.122 = (f32[4,64]{1,0:T(4,128)S(1)}, f32[4,64]{1,0:T(4,128)}, u32[]{:S(2)}) copy-start(f32[4,64]{1,0:T(4,128)} %copy-done.121) | copy-start | bytes 3076
  320.9 418.1 %reduce-scatter.24.cloned.1.call-start = ((), (), s32[]{:S(2)}) async-start(), calls=%async_computation.18 | async-start | bytes 3760128 | tf_op jit(solution)/shard_map/reduce_scatter | solution.py:487
  439.0 386.1 %reduce-scatter.26.cloned.1.call-start = ((), (), s32[]{:S(2)}) async-start(), calls=%async_computation.19 | async-start | bytes 5013504 | tf_op jit(solution)/shard_map/reduce_scatter | solution.py:487
  446.9 442.3 %reduce-scatter.20.cloned.1.call-start = ((), (), s32[]{:S(2)}) async-start(), calls=%async_computation.16 | async-start | bytes 69632 | tf_op jit(solution)/shard_map/reduce_scatter | solution.py:487
  525.4 16.7 %collective-permute-start.2 = (bf16[4,48,256]{2,1,0:T(8,128)(2,1)}, bf16[4,48,256]{2,1,0:T(8,128)(2,1)}, u32[]{:S(2)}, u32[]{:S(2)}) collective-permute-start(bf16[4,48,256]{2,1,0:T(8,128)(2,1)} %get-tuple-element.118), channel_id=1, source_target_pairs={{1,0},{2,1},{3,2},{4,3},{5,4},{6,5},{7,6},{8,7},{9,8},{10,9},{11,1... | collective-permute-start | bytes 294920 | tf_op jit(solution)/shard_map/ppermute | solution.py:37
  530.9 425.9 %reduce-scatter.18.cloned.1.call-start = ((), (), s32[]{:S(2)}) async-start(), calls=%async_computation.15 | async-start | bytes 139264 | tf_op jit(solution)/shard_map/reduce_scatter | solution.py:487
  539.0 4.7 collective-permute-start.3
  542.0 482.6 %reduce-scatter.16.cloned.1.call-start = ((), (), s32[]{:S(2)}) async-start(), calls=%async_computation.14 | async-start | bytes 139264 | tf_op jit(solution)/shard_map/reduce_scatter | solution.py:487
  548.1 542.6 %reduce-scatter.22.cloned.1.call-start = ((), (), s32[]{:S(2)}) async-start(), calls=%async_computation.17 | async-start | bytes 208896 | tf_op jit(solution)/shard_map/reduce_scatter | solution.py:487
  549.2 608.3 %reduce-scatter.14.cloned.1.call-start = ((), (), s32[]{:S(2)}) async-start(), calls=%async_computation.13 | async-start | bytes 208896 | tf_op jit(solution)/shard_map/reduce_scatter | solution.py:487
  555.3 686.5 %all-reduce.8.cloned.1.call-start = ((), (), s32[]{:S(2)}) async-start(), calls=%async_computation.23 | async-start | bytes 2064384 | tf_op jit(solution)/shard_map/psum | solution.py:483
  555.3 272.5 %copy-start.131 = (f32[4,256]{1,0:T(4,128)S(1)}, f32[4,256]{1,0:T(4,128)}, u32[]{:S(2)}) copy-start(f32[4,256]{1,0:T(4,128)} %get-tuple-element.45) | copy-start | bytes 12292
  555.4 272.5 %copy-start.130 = (f32[4,256]{1,0:T(4,128)S(1)}, f32[4,256]{1,0:T(4,128)}, u32[]{:S(2)}) copy-start(f32[4,256]{1,0:T(4,128)} %get-tuple-element.44) | copy-start | bytes 12292
  827.9 420.7 %copy-start.1 = (bf16[384,4608]{1,0:T(8,128)(2,1)S(1)}, bf16[384,4608]{1,0:T(8,128)(2,1)}, u32[]{:S(2)}) copy-start(bf16[384,4608]{1,0:T(8,128)(2,1)} %param.37) | copy-start | bytes 10616836
  (152 other events, 627.1 us)
Sparse Core Ops, SparseCore 0:
  66.4 97.1 all-gather.1
  307.4 119.9 reduce-scatter.11
  431.7 65.8 reduce-scatter.27
  501.4 71.3 reduce-scatter.31
  576.7 81.8 reduce-scatter.29
  663.0 75.8 reduce-scatter.23
  743.5 81.5 reduce-scatter.25
  828.7 60.4 reduce-scatter.19
  892.9 63.7 reduce-scatter.17
  960.8 63.8 reduce-scatter.15
  1028.4 62.3 reduce-scatter.21
  1094.9 62.4 reduce-scatter.13
  1160.3 81.3 all-reduce.7
where the time goes:
time: 1260 us
  waiting for transfers between devices  701 us (56%)
  matrix products  193 us (15%)
  other arithmetic  129 us (10%)
  local copies, waits for them, and re-layouts  104 us (8%)
  blocking collectives  104 us (8%)
  between operations  17 us (1%)
    reduce_scatter x10, waiting for transfers between devices, body(): lax.psum_scatter(for_sending(summed), 'seq', scatter_dimension=0, tiled=T...  528 us
    reduce_scatter x1, waiting for transfers between devices, token_backward(): lax.psum_scatter(grad_joined.astype(jnp.bfloat16), 'seq', scatter_dimensi...  95.8 us
    unnamed x1, blocking collectives  67.2 us
    psum x1, waiting for transfers between devices, body(): lax.psum(for_sending(all_grads), 'samp')  39 us
    all_gather x1, waiting for transfers between devices, token_forward(): gathered = lax.all_gather(joined, 'seq', axis=1, tiled=True)  38 us
    psum x1, blocking collectives, body(): lax.psum(for_sending(all_grads), 'samp')  36.5 us
    dot_general x1, matrix products, body(): jnp.einsum('cqk,hc->hqk', token_pair_low, token_w_pair, preferred_element...  27.7 us
    dot_general x1, matrix products, token_backward(): jnp.einsum('shqk,cqk->hc', grad_scores, pair_low, preferred_element_type=...  26.8 us
  transfers between devices with their start and end apart: 17, of which 11 were waited for; matrix products, arithmetic and copies ran while one was open for 18% of the time, Pallas kernels for 0%

commit v1 on v0

--- a/solution.py
+++ b/solution.py
@@ -395,6 +395,36 @@
     )
 
 
+def reduce_weights(grads):
+    runs, samples, cores = lax.axis_size("seq"), lax.axis_size("samp"), 2
+    lanes = 256
+    pieces = [g.astype(jnp.bfloat16).reshape(runs, -1) for g in grads]
+    lengths = [piece.shape[1] for piece in pieces]
+    flat = jnp.concatenate(pieces, axis=1)
+    unit = samples * 16 * lanes
+    padded = -(-flat.shape[1] // unit) * unit
+    flat = jnp.pad(flat, ((0, 0), (0, padded - flat.shape[1])))
+    rows = padded // (samples * lanes)
+    parts = flat.reshape(runs // cores, cores, samples, rows, lanes).transpose(1, 2, 0, 3, 4)
+    parts = parts.reshape(cores, samples * (runs // cores) * rows, lanes)
+    core_groups = [[i, i + 1] for i in range(0, runs, cores)]
+    met = lax.all_to_all(parts, "seq", 0, 0, tiled=True, axis_index_groups=core_groups)
+    chip = (met[0].astype(jnp.float32) + met[1].astype(jnp.float32)).astype(jnp.bfloat16)
+    chips = samples * runs // cores
+    chip_groups = [[c + cores * i for i in range(chips)] for c in range(cores)]
+    spread = lax.all_to_all(
+        chip.reshape(chips, rows, lanes), ("samp", "seq"), 0, 0, tiled=True, axis_index_groups=chip_groups
+    )
+    own = jnp.sum(spread.astype(jnp.float32), axis=0).astype(jnp.bfloat16)
+    copies = jnp.broadcast_to(own[None], (samples, rows, lanes))
+    total = lax.all_to_all(copies, "samp", 0, 0, tiled=True).reshape(-1)
+    shares, at = [], 0
+    for g, length in zip(grads, lengths):
+        shares.append(total[at : at + length].reshape(g.shape[0] // runs, -1).astype(jnp.float32))
+        at += length
+    return shares
+
+
 def body(
     atom_in,
     tok_in,
@@ -479,13 +509,7 @@
         grad_atom_out, atom_stored, atom_low, atom_weights, atom_bwd
     )
     all_grads = atom_grads + (weight_grad(pooled_low, grad_pool),) + token_grads
-    summed = jax.tree.map(
-        lambda part: part.astype(jnp.float32), lax.psum(for_sending(all_grads), "samp")
-    )
-    shares = jax.tree.map(
-        lambda part: part.astype(jnp.float32),
-        lax.psum_scatter(for_sending(summed), "seq", scatter_dimension=0, tiled=True),
-    )
+    shares = reduce_weights(all_grads)
     return (token_out.astype(jnp.bfloat16), grad_atoms, grad_start) + tuple(shares)
 
 

time: 1260 us -> 866 us (0.69)
  waiting for transfers between devices: 701 us -> 103 us
  local copies, waits for them, and re-layouts: 104 us -> 270 us
  blocking collectives: 104 us -> 132 us
    reduce_scatter x10 -> x0, waiting for transfers between devices: 528 us -> none  [body(): lax.psum_scatter(for_sending(summed), 'seq', scatter_dimension=0, tiled=T...]
    all_to_all x0 -> x2, blocking collectives: none -> 132 us  [the longest x1 113 us: reduce_weights(): lax.all_to_all(chip.reshape(chips, rows, lanes), ('samp', 'seq'), 0, 0, t...]
    unnamed x329 -> x381, local copies, waits for them, and re-layouts: 18.1 us -> 126 us
    unnamed x1 -> x0, blocking collectives: 67.2 us -> none
    reduce_scatter x1, waiting for transfers between devices: 95.8 us -> 50.4 us  [token_backward(): lax.psum_scatter(grad_joined.astype(jnp.bfloat16), 'seq', scatter_dimensi...]
    psum x1 -> x0, waiting for transfers between devices: 39 us -> none  [body(): lax.psum(for_sending(all_grads), 'samp')]
    psum x1 -> x0, blocking collectives: 36.5 us -> none  [body(): lax.psum(for_sending(all_grads), 'samp')]
    reshape x0 -> x11, local copies, waits for them, and re-layouts: none -> 27.5 us  [reduce_weights(): pieces = [g.astype(jnp.bfloat16).reshape(runs, -1) for g in grads]]
  transfers between devices with their start and end apart: 17 -> 7, of which waited for: 11 -> 3; matrix products, arithmetic and copies ran while one was open for 18% -> 18% of each run, Pallas kernels for 0% -> 0%
where the time goes in v1:
time: 866 us; the launch traced here: 857 us
  local copies, waits for them, and re-layouts  270 us (31%)
  matrix products  198 us (23%)
  blocking collectives  132 us (15%)
  other arithmetic  125 us (14%)
  waiting for transfers between devices  103 us (12%)
  between operations  16.8 us (2%)
  starting transfers between devices  12.2 us (1%)
    unnamed x381, local copies, waits for them, and re-layouts  126 us
    all_to_all x1, blocking collectives, reduce_weights(): lax.all_to_all(chip.reshape(chips, rows, lanes), ('samp', 'seq'), 0, 0, t...  113 us
    reduce_scatter x1, waiting for transfers between devices, token_backward(): lax.psum_scatter(grad_joined.astype(jnp.bfloat16), 'seq', scatter_dimensi...  50.4 us
    all_gather x1, waiting for transfers between devices, token_forward(): gathered = lax.all_gather(joined, 'seq', axis=1, tiled=True)  37.9 us
    dot_general x1, matrix products, token_backward(): jnp.einsum('shqk,cqk->hc', grad_scores, pair_low, preferred_element_type=...  33 us
    dot_general x1, matrix products, body(): jnp.einsum('cqk,hc->hqk', token_pair_low, token_w_pair, preferred_element...  27.8 us
    reshape x11, local copies, waits for them, and re-layouts, reduce_weights(): pieces = [g.astype(jnp.bfloat16).reshape(runs, -1) for g in grads]  27.5 us
    dot_general x11, matrix products, product(): return jnp.dot(left, right, preferred_element_type=jnp.float32)  22.7 us
  transfers between devices with their start and end apart: 7, of which 3 were waited for; matrix products, arithmetic and copies ran while one was open for 18% of the time, Pallas kernels for 0%

profile of v1, /device:TPU:0, one launch (start us, length us, event | category | flops | bytes accessed | tf_op | source)
XLA Modules:
  0.0 856.5 jit_solution(10849285210783907027)
XLA Ops:
  73.5 9.6 %fusion.2 = f32[64,1024]{1,0:T(8,128)S(1)} fusion(bf16[128,64,1024]{2,1,0:T(8,128)(2,1)} %param.29, f32[64,1024]{1,0:T(8,128)S(1)} %broadcast_multiply_fusion), kind=kLoop, calls=%fused_computation.12 | loop fusion | flops 33488896 | bytes 17301504 | tf_op jit(solution)/shard_map/reduce_sum | solution.py:68
  91.8 27.8 %fusion.32 = f32[16,64,1024]{2,0,1:T(8,128)S(1)} fusion(bf16[128,64,1024]{2,1,0:T(8,128)(2,1)} %fusion.3, bf16[16,128]{1,0:T(8,128)(2,1)S(1)} %copy-done.156), kind=kOutput, calls=%fused_computation.73 | convolution fusion | flops 268435456 | bytes 20975616 | tf_op jit(solution)/shard_map/cqk,hc->hqk/dot_general | solution.py:465
  124.4 37.9 %all-gather.2.cloned.1.call-done = bf16[4,1024,1536]{2,1,0:T(8,128)(2,1)} async-done(((bf16[4,64,1536]{2,1,0:T(8,128)(2,1)}), bf16[4,1024,1536]{2,1,0:T(8,128)(2,1)}) %all-gather.2.cloned.1.call-update) | async-done | bytes 12582928 | tf_op jit(solution)/shard_map/all_gather | solution.py:116
  162.3 10.3 %fusion.216 = (bf16[4,1024,768]{2,1,0:T(8,128)(2,1)}, bf16[4,1024,768]{2,1,0:T(8,128)(2,1)}) fusion(bf16[4,1024,1536]{2,1,0:T(8,128)(2,1)} %all-gather.2.cloned.1.call-done), kind=kLoop, calls=%fused_computation.412 | loop fusion | bytes 25165824 | tf_op jit(solution)/shard_map/slice | solution.py:117
  172.6 8.6 %copy.168 = bf16[4,1024,768]{1,2,0:T(8,128)(2,1)} copy(bf16[4,1024,768]{2,1,0:T(8,128)(2,1)} %get-tuple-element.56) | data formatting | bytes 12582912 | tf_op jit(solution)/shard_map/slice | solution.py:117
  181.2 12.4 %fusion.224 = (f32[4,16,64]{2,1,0:T(8,128)S(1)}, f32[4,16,64,1024]{3,2,1,0:T(8,128)}) fusion(f32[16,64,1024]{2,1,0:T(8,128)} %copy.171, bf16[4,64,16,48]{1,3,2,0:T(8,128)(2,1)S(1)} %bitcast.328, bf16[4,1024,16,48]{1,3,2,0:T(8,128)(2,1)} %bitcast.297), kind=kOutput, calls=%fused_computation.420 | convolution fusion | flops 415232000 | bytes 27672576 | tf_op jit(solution)/shard_map/sqhd,skhd->shqk/dot_general | solution.py:106
  209.6 10.6 %fusion.13 = f32[4,16,48,64]{3,2,1,0:T(8,128)} fusion(bf16[4,1024,16,48]{1,3,2,0:T(8,128)(2,1)} %bitcast.306, f32[4,16,64,1024]{3,2,1,0:T(8,128)} %get-tuple-element.121, f32[4,16,64]{2,1,0:T(8,128)S(1)} %fusion.4, f32[4,16,64]{2,1,0:T(8,128)S(1)} %get-tuple-element.120), kind=kOutput, calls=%fused_computation.48 | convolution fusion | flops 415236096 | bytes 23887872 | tf_op jit(solution)/shard_map/shqk,skhd->sqhd/dot_general | solution.py:125
  238.9 13.8 %multiply_reduce_fusion = (f32[4,16,64]{2,1,0:T(8,128)S(1)}, f32[4,16,64,1024]{3,2,1,0:T(8,128)}) fusion(f32[4,16,64,1024]{3,2,1,0:T(8,128)} %get-tuple-element.121, f32[4,16,64]{2,1,0:T(8,128)S(1)} %log_add_fusion.1, bf16[4,64,16,48]{1,3,2,0:T(8,128)(2,1)S(1)} %bitcast.318, bf16[4,1024,16,48]{1,3,2,0:T(8,128)(2,1)} %bitcast.307), kind=kOutput, calls=%fused_computation.17 | convolution fusion | flops 415232000 | bytes 40271872 | tf_op jit(solution)/shard_map/sqhd,skhd->shqk/dot_general | solution.py:142
  252.7 9.0 %fusion.23 = bf16[4,16,48,1024]{3,2,1,0:T(8,128)(2,1)} fusion(bf16[4,64,16,48]{1,3,2,0:T(8,128)(2,1)S(1)} %bitcast.319, f32[4,16,64,1024]{3,2,1,0:T(8,128)} %get-tuple-element.121, f32[4,16,64]{2,1,0:T(8,128)S(1)} %log_add_fusion.1), kind=kOutput, calls=%fused_computation.62 | convolution fusion | flops 414187520 | bytes 23478272 | tf_op jit(solution)/shard_map/shqk,sqhd->skhd/dot_general | solution.py:155
  261.7 14.1 %convert_reduce_fusion.1 = (bf16[16,64,1024]{2,1,0:T(8,128)(2,1)}, bf16[4,16,64,1024]{3,2,1,0:T(8,128)(2,1)S(1)}) fusion(f32[4,16,64,1024]{3,2,1,0:T(8,128)} %get-tuple-element.126, f32[4,16,64]{2,1,0:T(8,128)S(1)} %get-tuple-element.125, f32[4,16,64,1024]{3,2,1,0:T(8,128)} %get-tuple-element.121, f32[4,16,64]{2,1,0:T(8,128)S(1)} %log_add_fusion.1), kind=kLoop, calls=%fused_computation.15 | loop fusion | flops 24117248 | bytes 44072960 | tf_op jit(solution)/shard_map/shqk,cqk->hc/reduce_sum | solution.py:161
  289.6 8.6 %copy.177 = bf16[4,1024,768]{2,1,0:T(8,128)(2,1)} copy(bf16[4,1024,768]{1,2,0:T(8,128)(2,1)} %bitcast.304) | data formatting | bytes 12582912 | tf_op jit(solution)/shard_map/reshape | solution.py:167
  298.2 10.4 %pad_maximum_fusion = bf16[4,1024,1536]{2,1,0:T(8,128)(2,1)} fusion(bf16[4,1024,768]{2,1,0:T(8,128)(2,1)} %copy.177, bf16[4,1024,768]{2,1,0:T(8,128)(2,1)} %copy.176), kind=kLoop, calls=%fused_computation.28 | loop fusion | flops 25165824 | bytes 25165824 | tf_op jit(solution)/shard_map/concatenate | solution.py:164
  313.6 9.5 %multiply_convert_fusion.4 = bf16[4,16,48,64]{3,2,1,0:T(8,128)(2,1)S(1)} fusion(bf16[4,1024,16,48]{1,3,2,0:T(8,128)(2,1)} %bitcast.298, bf16[4,16,64,1024]{3,2,1,0:T(8,128)(2,1)} %copy-done.2), kind=kOutput, calls=%fused_computation.90 | convolution fusion | flops 403046400 | bytes 15073280 | tf_op jit(solution)/shard_map/shqk,skhd->sqhd/dot_general | solution.py:148
  345.3 33.0 %fusion.54 = bf16[16,128]{1,0:T(8,128)(2,1)} fusion(bf16[128,64,1024]{2,1,0:T(8,128)(2,1)} %fusion.3, bf16[16,64,1024]{2,1,0:T(8,128)(2,1)S(1)} %copy-done.67), kind=kOutput, calls=%fused_computation.120 | convolution fusion | flops 268435456 | bytes 18878464 | tf_op jit(solution)/shard_map/shqk,cqk->hc/dot_general | solution.py:161
  378.3 50.4 %reduce-scatter.2.cloned.1.call-done = bf16[4,64,1536]{2,1,0:T(8,128)(2,1)} async-done(((bf16[4,1024,1536]{2,1,0:T(8,128)(2,1)}), bf16[4,64,1536]{2,1,0:T(8,128)(2,1)}) %reduce-scatter.2.cloned.1.call-update) | async-done | bytes 786448 | tf_op jit(solution)/shard_map/reduce_scatter | solution.py:171
  544.8 18.6 %dynamic-update-slice.13 = bf16[16,539780]{1,0:T(8,128)(2,1)} dynamic-update-slice(bf16[16,539780]{1,0:T(8,128)(2,1)} %dynamic-update-slice.12, bf16[16,110592]{1,0:T(8,128)(2,1)S(1)} %copy-done.10, s32[]{} %constant.159, s32[]{} %constant.166) | dynamic-update-slice | bytes 7077892
  563.5 26.3 %dynamic-update-slice.14 = bf16[16,539780]{1,0:T(8,128)(2,1)} dynamic-update-slice(bf16[16,539780]{1,0:T(8,128)(2,1)} %dynamic-update-slice.13, bf16[16,147456]{1,0:T(8,128)(2,1)} %reshape.511, s32[]{} %constant.159, s32[]{} %constant.167) | dynamic-update-slice | bytes 9437188
  597.3 26.4 %dynamic-update-slice.16 = bf16[16,539780]{1,0:T(8,128)(2,1)} dynamic-update-slice(bf16[16,539780]{1,0:T(8,128)(2,1)} %dynamic-update-slice.15, bf16[16,147456]{1,0:T(8,128)(2,1)} %reshape.513, s32[]{} %constant.159, s32[]{} %constant.169) | dynamic-update-slice | bytes 9437188
  623.7 13.3 %dynamic-update-slice.17 = bf16[16,539780]{1,0:T(8,128)(2,1)} dynamic-update-slice(bf16[16,539780]{1,0:T(8,128)(2,1)} %dynamic-update-slice.16, bf16[16,73728]{1,0:T(8,128)(2,1)S(1)} %copy-done.12, s32[]{} %constant.159, s32[]{} %constant.170) | dynamic-update-slice | bytes 4718596
  638.5 10.7 %pad.8 = bf16[16,557056]{1,0:T(8,128)(2,1)S(1)} pad(bf16[16,539780]{1,0:T(8,128)(2,1)} %dynamic-update-slice.18, bf16[]{:T(256)} %constant.153.clone.1), padding=0_0x0_17276 | pad | bytes 35098752 | tf_op jit(solution)/shard_map/jit(_pad)/pad | solution.py:406
  649.2 12.3 %copy.221 = bf16[2,8,2176,256]{3,2,1,0:T(8,128)(2,1)S(1)} copy(bf16[2,8,2176,256]{3,1,2,0:T(8,128)(2,1)S(1)} %bitcast.299) | data formatting | bytes 35651584
  664.3 18.9 %all_to_all.15 = bf16[2,17408,256]{2,1,0:T(8,128)(2,1)S(1)} all-to-all(bf16[2,17408,256]{2,1,0:T(8,128)(2,1)S(1)} %bitcast.301), channel_id=1, replica_groups={{0,1},{2,3},{4,5},{6,7},{8,9},{10,11},{12,13},{14,15},{16,17},{18,19},{..., dimensions={0} | all-to-all | bytes 35651584 | tf_op jit(solution)/shard_map/all_to_all | solution.py:411
  685.8 112.7 %all_to_all.16 = bf16[64,272,256]{2,1,0:T(8,128)(2,1)} all-to-all(bf16[64,272,256]{2,1,0:T(8,128)(2,1)S(1)} %bitcast.305), channel_id=1, replica_groups={{0,2,4,6,8,10,12,14,16,18,20,22,24,26,28,30,32,34,36,38,40,42,44,46,48,..., dimensions={0} | all-to-all | bytes 17825792 | tf_op jit(solution)/shard_map/all_to_all | solution.py:415
  809.9 14.1 %all-to-all-done.2 = bf16[8,272,256]{2,1,0:T(8,128)(2,1)S(1)} async-done(((bf16[8,272,256]{2,1,0:T(8,128)(2,1)}), bf16[8,272,256]{2,1,0:T(8,128)(2,1)S(1)}, u32[]{:S(2)}, u32[]{:S(2)}) %all-to-all-start.2) | async-done | bytes 1114144 | tf_op jit(solution)/shard_map/all_to_all | solution.py:420
  (590 shorter events, 320.2 us)
Async XLA Ops:
  7.2 15.7 %copy-start = (bf16[384,4608]{1,0:T(8,128)(2,1)S(1)}, bf16[384,4608]{1,0:T(8,128)(2,1)}, u32[]{:S(2)}) copy-start(bf16[384,4608]{1,0:T(8,128)(2,1)} %param.37) | copy-start | bytes 10616836
  7.2 155.1 %all-gather.2.cloned.1.call-start = ((), (), s32[]{:S(2)}) async-start(), calls=%async_computation.4 | async-start | bytes 13369344 | tf_op jit(solution)/shard_map/all_gather | solution.py:116
  15.9 16.4 %collective-permute-start = (bf16[4,48,256]{2,1,0:T(8,128)(2,1)}, bf16[4,48,256]{2,1,0:T(8,128)(2,1)}, u32[]{:S(2)}, u32[]{:S(2)}) collective-permute-start(bf16[4,48,256]{2,1,0:T(8,128)(2,1)} %get-tuple-element.93), channel_id=1, source_target_pairs={{0,1},{1,2},{2,3},{3,4},{4,5},{5,6},{6,7},{7,8},{8,9},{9,10},{10,1... | collective-permute-start | bytes 294920 | tf_op jit(solution)/shard_map/ppermute | solution.py:25
  17.9 14.5 %collective-permute-start.1 = (bf16[4,48,256]{2,1,0:T(8,128)(2,1)}, bf16[4,48,256]{2,1,0:T(8,128)(2,1)}, u32[]{:S(2)}, u32[]{:S(2)}) collective-permute-start(bf16[4,48,256]{2,1,0:T(8,128)(2,1)} %get-tuple-element.94), channel_id=1, source_target_pairs={{1,0},{2,1},{3,2},{4,3},{5,4},{6,5},{7,6},{8,7},{9,8},{10,9},{11,1... | collective-permute-start | bytes 294920 | tf_op jit(solution)/shard_map/ppermute | solution.py:27
  25.8 32.4 %copy-start.68 = (f32[64,768]{1,0:T(8,128)}, f32[64,768]{1,0:T(8,128)S(1)}, u32[]{:S(2)}) copy-start(f32[64,768]{1,0:T(8,128)S(1)} %get-tuple-element.85) | copy-start | bytes 589828
  64.9 363.8 %reduce-scatter.2.cloned.1.call-start = ((), (), s32[]{:S(2)}) async-start(), calls=%async_computation.5 | async-start | bytes 13369344 | tf_op jit(solution)/shard_map/reduce_scatter | solution.py:171
  65.0 18.2 %slice-start = ((s8[16777216]{0:T(1024)(128)(4,1)}), s8[4194304]{0:T(1024)(128)(4,1)S(1)}, s32[]{:S(2)}) async-start(s8[16777216]{0:T(1024)(128)(4,1)} %bitcast.295), calls=%async_computation.6 | async-start | bytes 8388608
  65.0 18.2 %slice-start.1 = ((s8[16777216]{0:T(1024)(128)(4,1)}), s8[4194304]{0:T(1024)(128)(4,1)S(1)}, s32[]{:S(2)}) async-start(s8[16777216]{0:T(1024)(128)(4,1)} %bitcast.295), calls=%async_computation.7 | async-start | bytes 8388608
  124.4 56.9 %copy-start.42 = (bf16[4,64,768]{1,2,0:T(8,128)(2,1)}, bf16[4,64,768]{1,2,0:T(8,128)(2,1)S(1)}, u32[]{:S(2)}) copy-start(bf16[4,64,768]{1,2,0:T(8,128)(2,1)S(1)} %copy.218) | copy-start | bytes 1179652
  261.7 14.1 %copy-start.43 = (bf16[4,64,768]{1,2,0:T(8,128)(2,1)S(1)}, bf16[4,64,768]{1,2,0:T(8,128)(2,1)}, u32[]{:S(2)}) copy-start(bf16[4,64,768]{1,2,0:T(8,128)(2,1)} %copy-done.42) | copy-start | bytes 1179652
  313.6 10.5 %copy-start.94 = (f32[64,768]{1,0:T(8,128)S(1)}, f32[64,768]{1,0:T(8,128)}, u32[]{:S(2)}) copy-start(f32[64,768]{1,0:T(8,128)} %get-tuple-element.86) | copy-start | bytes 589828
  345.2 83.5 %copy-start.69 = (f32[64,768]{1,0:T(8,128)S(1)}, f32[64,768]{1,0:T(8,128)}, u32[]{:S(2)}) copy-start(f32[64,768]{1,0:T(8,128)} %copy-done.68) | copy-start | bytes 589828
  345.2 83.5 %copy-start.115 = (bf16[4,64,768]{2,1,0:T(8,128)(2,1)S(1)}, bf16[4,64,768]{2,1,0:T(8,128)(2,1)}, u32[]{:S(2)}) copy-start(bf16[4,64,768]{2,1,0:T(8,128)(2,1)} %copy.178) | copy-start | bytes 1179652
  345.2 83.5 %copy-start.138 = (f32[4,64]{1,0:T(4,128)S(1)}, f32[4,64]{1,0:T(4,128)}, u32[]{:S(2)}) copy-start(f32[4,64]{1,0:T(4,128)} %copy-done.137) | copy-start | bytes 3076
  345.2 83.5 %copy-start.142 = (f32[4,64]{1,0:T(4,128)S(1)}, f32[4,64]{1,0:T(4,128)}, u32[]{:S(2)}) copy-start(f32[4,64]{1,0:T(4,128)} %copy-done.141) | copy-start | bytes 3076
  510.2 12.7 %collective-permute-start.2 = (bf16[4,48,256]{2,1,0:T(8,128)(2,1)}, bf16[4,48,256]{2,1,0:T(8,128)(2,1)}, u32[]{:S(2)}, u32[]{:S(2)}) collective-permute-start(bf16[4,48,256]{2,1,0:T(8,128)(2,1)} %get-tuple-element.108), channel_id=1, source_target_pairs={{1,0},{2,1},{3,2},{4,3},{5,4},{6,5},{7,6},{8,7},{9,8},{10,9},{11,1... | collective-permute-start | bytes 294920 | tf_op jit(solution)/shard_map/ppermute | solution.py:37
  511.5 12.4 %collective-permute-start.3 = (bf16[4,48,256]{2,1,0:T(8,128)(2,1)}, bf16[4,48,256]{2,1,0:T(8,128)(2,1)}, u32[]{:S(2)}, u32[]{:S(2)}) collective-permute-start(bf16[4,48,256]{2,1,0:T(8,128)(2,1)} %get-tuple-element.107), channel_id=1, source_target_pairs={{0,1},{1,2},{2,3},{3,4},{4,5},{5,6},{6,7},{7,8},{8,9},{9,10},{10,1... | collective-permute-start | bytes 294920 | tf_op jit(solution)/shard_map/ppermute | solution.py:37
  530.2 10.9 %copy-start.146 = (bf16[16,4]{1,0:T(8,128)(2,1)S(1)}, bf16[16,4]{1,0:T(8,128)(2,1)}, u32[]{:S(2)}) copy-start(bf16[16,4]{1,0:T(8,128)(2,1)} %copy.204) | copy-start | bytes 388
  530.3 14.6 %copy-start.10 = (bf16[16,110592]{1,0:T(8,128)(2,1)S(1)}, bf16[16,110592]{1,0:T(8,128)(2,1)}, u32[]{:S(2)}) copy-start(bf16[16,110592]{1,0:T(8,128)(2,1)} %reshape.510) | copy-start | bytes 10616836
  563.5 26.4 %copy-start.44 = (bf16[16,36864]{1,0:T(8,128)(2,1)S(1)}, bf16[16,36864]{1,0:T(8,128)(2,1)}, u32[]{:S(2)}) copy-start(bf16[16,36864]{1,0:T(8,128)(2,1)} %reshape.512) | copy-start | bytes 3538948
  597.3 26.4 %copy-start.12 = (bf16[16,73728]{1,0:T(8,128)(2,1)S(1)}, bf16[16,73728]{1,0:T(8,128)(2,1)}, u32[]{:S(2)}) copy-start(bf16[16,73728]{1,0:T(8,128)(2,1)} %reshape.514) | copy-start | bytes 7077892
  623.7 13.3 %copy-start.155 = (bf16[16,128]{1,0:T(8,128)(2,1)S(1)}, bf16[16,128]{1,0:T(8,128)(2,1)}, u32[]{:S(2)}) copy-start(bf16[16,128]{1,0:T(8,128)(2,1)} %fusion.54) | copy-start | bytes 12292
  804.6 19.4 %all-to-all-start.2 = ((bf16[8,272,256]{2,1,0:T(8,128)(2,1)}), bf16[8,272,256]{2,1,0:T(8,128)(2,1)S(1)}, u32[]{:S(2)}, u32[]{:S(2)}) async-start(bf16[8,272,256]{2,1,0:T(8,128)(2,1)} %broadcast_in_dim.32), calls=%async_computation.3 | async-start | bytes 2228224 | tf_op jit(solution)/shard_map/all_to_all | solution.py:420
  835.2 14.2 %copy-start.1 = (bf16[384,4608]{1,0:T(8,128)(2,1)S(1)}, bf16[384,4608]{1,0:T(8,128)(2,1)}, u32[]{:S(2)}) copy-start(bf16[384,4608]{1,0:T(8,128)(2,1)} %param.37) | copy-start | bytes 10616836
  (163 other events, 555.7 us)
Sparse Core Ops, SparseCore 0:
  65.0 97.1 all-gather.1
  308.8 119.9 reduce-scatter.1
